TPU v7x, 256 devices: a whole 4x4x8 slice. The times are simulated.
256 devices in a mesh: dp: 4 (over z_lo, core), expert: 64 (over x, y, z_hi).
Axes of the slice: x: 4, y: 4, z: 8 (z_hi: 4, z_lo: 2; z = z_hi * 2 + z_lo), core: 2. Of those that a mesh axis runs over, the one named last changes fastest.
Arguments:
- tokens: bfloat16 [32768, 2048], P(('dp', 'expert')), may hold values from -6 to 6
- d_out: bfloat16 [32768, 2048], P(('dp', 'expert')), may hold values from -6 to 6
- route_probs: bfloat16 [32768, 8], P(('dp', 'expert')), may hold values from 0.019897461 to 0.3984375
- routes: int32 [32768, 8], P(('dp', 'expert')), may hold values from 0 to 63, all different within a row; in each aligned block of 128 rows (0 to 127, 128 to 255, ...) at most 17 rows name the same one
- w_gate: bfloat16 [64, 2048, 512], P('expert'), may hold values from -0.125 to 0.125
- w_up: bfloat16 [64, 2048, 512], P('expert'), may hold values from -0.125 to 0.125
- w_down: bfloat16 [64, 512, 2048], P('expert'), may hold values from -0.25 to 0.25
Outputs:
- d_tokens: bfloat16 [32768, 2048], P(('dp', 'expert'))
- d_probs: bfloat16 [32768, 8], P(('dp', 'expert'))
- grad_gate: bfloat16 [64, 2048, 512], P('expert', 'dp')
- grad_up: bfloat16 [64, 2048, 512], P('expert', 'dp')
- grad_down: bfloat16 [64, 512, 2048], P('expert', None, 'dp')
Inputs may be any that keep to these rules, and one draw needn't show every extreme that they name: `routes`: each row names 8 different experts. In the rows of one device each expert is named by at most 17 rows, a bound that some block reaches.
All inputs are finite; a program needn't handle non-finite values.
Results may differ from a plain program's by a relative error of at most 0.013.
Values may be sent and summed in bfloat16 or wider, within the bound.
A program may use at most 128 MiB of HBM per device.

v0:
```python
import jax
import jax.numpy as jnp
from jax import lax
from jax.sharding import PartitionSpec as P


def contract(left, right, left_dim, right_dim):
    return lax.dot_general(
        left, right, (((left_dim,), (right_dim,)), ((), ())), preferred_element_type=jnp.float32
    )


def shards(tokens, d_out, route_probs, routes, w_gate, w_up, w_down):
    tok_rows, model_width = tokens.shape
    top_count = routes.shape[1]
    experts = lax.axis_size("expert") * w_gate.shape[0]
    capacity = min(tok_rows, tok_rows * top_count // experts + 1)
    pairs = tok_rows * top_count
    total_rows = experts * capacity
    flat_routes = routes.reshape(pairs)
    onehot = (flat_routes[:, None] == jnp.arange(experts, dtype=jnp.int32)[None, :]).astype(
        jnp.int32
    )
    before = jnp.cumsum(onehot, axis=0) - onehot
    slot_index = jnp.sum(before * onehot, axis=1)
    target = flat_routes * capacity + slot_index
    assign = (
        jnp.full((total_rows,), pairs, jnp.int32).at[target].set(jnp.arange(pairs, dtype=jnp.int32))
    )
    owner = assign // top_count
    blank_row = jnp.zeros((1, model_width), jnp.bfloat16)
    x_send = jnp.concatenate([tokens, blank_row], axis=0)[owner].reshape(
        experts, capacity, model_width
    )
    dy_send = jnp.concatenate([d_out, blank_row], axis=0)[owner].reshape(
        experts, capacity, model_width
    )
    p_send = jnp.concatenate([route_probs.reshape(pairs), jnp.zeros((1,), jnp.bfloat16)])[
        assign
    ].reshape(experts, capacity)
    x_recv, p_recv = (
        lax.all_to_all(x_send, "expert", split_axis=0, concat_axis=0, tiled=True),
        lax.all_to_all(p_send, "expert", split_axis=0, concat_axis=0, tiled=True),
    )
    gate_w = w_gate[0]
    up_w = w_up[0]
    down_w = w_down[0]
    x_rows = x_recv.reshape(total_rows, model_width)
    gate_val = jnp.dot(x_rows, gate_w, preferred_element_type=jnp.float32)
    up_val = jnp.dot(x_rows, up_w, preferred_element_type=jnp.float32)
    sigmoid_g = jax.nn.sigmoid(gate_val)
    silu_g = gate_val * sigmoid_g
    hidden = (silu_g * up_val).astype(jnp.bfloat16)
    dy_recv = lax.all_to_all(dy_send, "expert", split_axis=0, concat_axis=0, tiled=True)
    dy_rows = dy_recv.reshape(total_rows, model_width)
    prob_col = p_recv.reshape(total_rows, 1).astype(jnp.float32)
    back_hidden = contract(dy_rows, down_w, 1, 1)
    prob_rows_grad = jnp.sum(hidden.astype(jnp.float32) * back_hidden, axis=1).astype(jnp.bfloat16)
    scaled_dy = (prob_col * dy_rows.astype(jnp.float32)).astype(jnp.bfloat16)
    grad_down_part = contract(hidden, scaled_dy, 0, 0)
    d_hidden = prob_col * back_hidden
    d_gate = (d_hidden * up_val * sigmoid_g * (1.0 + gate_val * (1.0 - sigmoid_g))).astype(
        jnp.bfloat16
    )
    d_up = (d_hidden * silu_g).astype(jnp.bfloat16)
    d_rows = (contract(d_gate, gate_w, 1, 1) + contract(d_up, up_w, 1, 1)).astype(jnp.bfloat16)
    grad_gate_part = contract(x_rows, d_gate, 0, 0)
    grad_up_part = contract(x_rows, d_up, 0, 0)
    d_back, prob_back = (
        lax.all_to_all(
            d_rows.reshape(experts, capacity, model_width),
            "expert",
            split_axis=0,
            concat_axis=0,
            tiled=True,
        ),
        lax.all_to_all(
            prob_rows_grad.reshape(experts, capacity),
            "expert",
            split_axis=0,
            concat_axis=0,
            tiled=True,
        ),
    )
    gate_sum, up_sum, grad_down_sum = (
        lax.psum_scatter(
            grad_gate_part.astype(jnp.bfloat16), "dp", scatter_dimension=0, tiled=True
        ).astype(jnp.float32),
        lax.psum_scatter(
            grad_up_part.astype(jnp.bfloat16), "dp", scatter_dimension=0, tiled=True
        ).astype(jnp.float32),
        lax.psum_scatter(
            grad_down_part.astype(jnp.bfloat16), "dp", scatter_dimension=1, tiled=True
        ).astype(jnp.float32),
    )
    per_pair = d_back.reshape(total_rows, model_width)[target]
    d_tokens = jnp.sum(
        per_pair.reshape(tok_rows, top_count, model_width).astype(jnp.float32), axis=1
    ).astype(jnp.bfloat16)
    d_probs = prob_back.reshape(total_rows)[target].reshape(tok_rows, top_count)
    return (
        d_tokens,
        d_probs,
        gate_sum.astype(jnp.bfloat16)[None],
        up_sum.astype(jnp.bfloat16)[None],
        grad_down_sum.astype(jnp.bfloat16)[None],
    )


def solution(mesh):
    return jax.shard_map(
        shards,
        mesh=mesh,
        in_specs=(
            P(("dp", "expert"), None),
            P(("dp", "expert"), None),
            P(("dp", "expert"), None),
            P(("dp", "expert"), None),
            P("expert", None, None),
            P("expert", None, None),
            P("expert", None, None),
        ),
        out_specs=(
            P(("dp", "expert"), None),
            P(("dp", "expert"), None),
            P("expert", "dp", None),
            P("expert", "dp", None),
            P("expert", None, "dp"),
        ),
        check_vma=False,
    )
```

profile of v0, /device:TPU:1, one launch (start us, length us, event | category | flops | bytes accessed | tf_op | source)
XLA Modules:
  0.0 637.9 jit_solution(8795708040502681043)
XLA Ops:
  10.1 18.0 %reduce-window.6 = s32[64,8,128]{2,1,0:T(8,128)S(1)} reduce-window(s32[64,8,128]{2,1,0:T(8,128)S(1)} %fusion.17, s32[]{:T(128)} %constant.13.clone.1), window={size=1x1x128 pad=0_0x0_0x127_0}, to_apply=%region_0.0 | reduce-window | flops 8323072 | bytes 524292 | tf_op jit(solution)/shard_map/reduce-window
  33.2 6.9 %gather_fusion = bf16[1088]{0:T(1024)(128)(2,1)S(1)} fusion(bf16[1025]{0:T(1024)(128)(2,1)S(1)} %pad_maximum_fusion, s32[2048]{0:T(1024)S(1)} %get-tuple-element.22), kind=kCustom, calls=%fused_computation | custom fusion | bytes 8704 | tf_op jit(solution)/shard_map/gather | solution.py:38
  40.9 15.1 %all-to-all-start = ((bf16[64,1,17]{2,1,0:T(2,128)(2,1)}), bf16[64,1,17]{2,1,0:T(2,128)(2,1)S(1)}, u32[]{:S(2)}, u32[]{:S(2)}) async-start(bf16[64,1,17]{2,1,0:T(2,128)(2,1)} %all_to_all.25), calls=%async_computation | async-start | bytes 65536 | tf_op jit(solution)/shard_map/all_to_all | solution.py:43
  56.1 5.8 gather_fusion.2
  61.9 7.6 %reshape.121 = bf16[64,17,2048]{2,1,0:T(8,128)(2,1)} reshape(bf16[1088,2048]{1,0:T(8,128)(2,1)} %gather_fusion.2) | data formatting | bytes 8912896 | tf_op jit(solution)/shard_map/reshape | solution.py:32
  69.6 12.5 %all-to-all-start.2 = ((bf16[64,17,2048]{2,1,0:T(8,128)(2,1)}), bf16[64,17,2048]{2,1,0:T(8,128)(2,1)}, u32[]{:S(2)}, u32[]{:S(2)}) async-start(bf16[64,17,2048]{2,1,0:T(8,128)(2,1)} %reshape.121), calls=%async_computation.2 | async-start | bytes 12582912 | tf_op jit(solution)/shard_map/all_to_all | solution.py:42
  82.2 5.9 gather_fusion.1
  88.0 7.6 %reshape.119 = bf16[64,17,2048]{2,1,0:T(8,128)(2,1)} reshape(bf16[1088,2048]{1,0:T(8,128)(2,1)} %gather_fusion.1) | data formatting | bytes 8912896 | tf_op jit(solution)/shard_map/reshape | solution.py:35
  95.7 123.0 %all-to-all-done.2 = bf16[64,17,2048]{2,1,0:T(8,128)(2,1)} async-done(((bf16[64,17,2048]{2,1,0:T(8,128)(2,1)}), bf16[64,17,2048]{2,1,0:T(8,128)(2,1)}, u32[]{:S(2)}, u32[]{:S(2)}) %all-to-all-start.2) | async-done | bytes 4456480 | tf_op jit(solution)/shard_map/all_to_all | solution.py:42
  218.7 11.5 %all-to-all-start.1 = ((bf16[64,17,2048]{2,1,0:T(8,128)(2,1)}), bf16[64,17,2048]{2,1,0:T(8,128)(2,1)}, u32[]{:S(2)}, u32[]{:S(2)}) async-start(bf16[64,17,2048]{2,1,0:T(8,128)(2,1)} %reshape.119), calls=%async_computation.1 | async-start | bytes 12582912 | tf_op jit(solution)/shard_map/all_to_all | solution.py:54
  230.7 7.7 %reshape.122 = bf16[1088,2048]{1,0:T(8,128)(2,1)} reshape(bf16[64,17,2048]{2,1,0:T(8,128)(2,1)} %all-to-all-done.2) | data formatting | bytes 8912896 | tf_op jit(solution)/shard_map/reshape | solution.py:48
  238.5 6.2 fusion.7
  248.6 130.0 %all-to-all-done.1 = bf16[64,17,2048]{2,1,0:T(8,128)(2,1)} async-done(((bf16[64,17,2048]{2,1,0:T(8,128)(2,1)}), bf16[64,17,2048]{2,1,0:T(8,128)(2,1)}, u32[]{:S(2)}, u32[]{:S(2)}) %all-to-all-start.1) | async-done | bytes 4456480 | tf_op jit(solution)/shard_map/all_to_all | solution.py:54
  378.6 7.7 %reshape.120 = bf16[1088,2048]{1,0:T(8,128)(2,1)} reshape(bf16[64,17,2048]{2,1,0:T(8,128)(2,1)} %all-to-all-done.1) | data formatting | bytes 8912896 | tf_op jit(solution)/shard_map/reshape | solution.py:55
  386.3 9.2 %multiply_reduce_fusion = (bf16[1088]{0:T(1024)(128)(2,1)S(1)}, bf16[1088,512]{1,0:T(8,128)(2,1)S(1)}, bf16[1088,512]{1,0:T(8,128)(2,1)}, bf16[1088,512]{1,0:T(8,128)(2,1)}) fusion(f32[1088,512]{1,0:T(8,128)} %fusion.10, f32[1088,512]{1,0:T(8,128)} %fusion.7, f32[1088]{0:T(1024)S(1)} %reshape.128, bf16[1088,2048]{1,0:T(8,128)(2,1)} %reshape.120, ...), kind=kOutput, calls=%fused_computation.15 | convolution fusion | flops 2292284416 | bytes 14358912 | tf_op jit(solution)/shard_map/dot_general | solution.py:8
  415.1 7.7 %reshape.123 = bf16[64,17,2048]{2,1,0:T(8,128)(2,1)} reshape(bf16[1088,2048]{1,0:T(8,128)(2,1)} %fusion) | data formatting | bytes 8912896 | tf_op jit(solution)/shard_map/reshape | solution.py:71
  422.7 12.3 %all-to-all-start.3 = ((bf16[64,17,2048]{2,1,0:T(8,128)(2,1)}), bf16[64,17,2048]{2,1,0:T(8,128)(2,1)}, u32[]{:S(2)}, u32[]{:S(2)}) async-start(bf16[64,17,2048]{2,1,0:T(8,128)(2,1)} %reshape.123), calls=%async_computation.3 | async-start | bytes 12582912 | tf_op jit(solution)/shard_map/all_to_all | solution.py:70
  435.1 6.9 %convolution_convert_fusion = bf16[2048,512]{1,0:T(8,128)(2,1)} fusion(bf16[1088,2048]{1,0:T(8,128)(2,1)} %reshape.122, bf16[1088,512]{1,0:T(8,128)(2,1)} %get-tuple-element.18), kind=kOutput, calls=%fused_computation.13 | convolution fusion | flops 2282749952 | bytes 7667712 | tf_op jit(solution)/shard_map/dot_general | solution.py:8
  442.3 6.5 %convolution_convert_fusion.1 = bf16[2048,512]{1,0:T(8,128)(2,1)} fusion(bf16[1088,2048]{1,0:T(8,128)(2,1)} %reshape.122, bf16[1088,512]{1,0:T(8,128)(2,1)S(1)} %copy-done.8), kind=kOutput, calls=%fused_computation.14 | convolution fusion | flops 2282749952 | bytes 7667712 | tf_op jit(solution)/shard_map/dot_general | solution.py:8
  449.2 6.8 %gather_fusion.4 = bf16[1024]{0:T(1024)(128)(2,1)S(1)} fusion(bf16[1088]{0:T(1024)(128)(2,1)S(1)} %reshape.126, s32[1024]{0:T(1024)S(1)} %broadcast_clamp_fusion), kind=kCustom, calls=%fused_computation.4 | custom fusion | bytes 8192 | tf_op jit(solution)/shard_map/gather | solution.py:100
  456.7 149.1 %all-to-all-done.3 = bf16[64,17,2048]{2,1,0:T(8,128)(2,1)} async-done(((bf16[64,17,2048]{2,1,0:T(8,128)(2,1)}), bf16[64,17,2048]{2,1,0:T(8,128)(2,1)}, u32[]{:S(2)}, u32[]{:S(2)}) %all-to-all-start.3) | async-done | bytes 4456480 | tf_op jit(solution)/shard_map/all_to_all | solution.py:70
  605.8 7.8 %reshape.124 = bf16[1088,2048]{1,0:T(8,128)(2,1)} reshape(bf16[64,17,2048]{2,1,0:T(8,128)(2,1)} %all-to-all-done.3) | data formatting | bytes 8912896 | tf_op jit(solution)/shard_map/reshape | solution.py:96
  613.6 11.8 %gather_fusion.3 = bf16[1024,2048]{1,0:T(8,128)(2,1)} fusion(bf16[1088,2048]{1,0:T(8,128)(2,1)} %reshape.124, s32[1024]{0:T(1024)S(1)} %broadcast_clamp_fusion), kind=kCustom, calls=%fused_computation.3 | custom fusion | bytes 8392704 | tf_op jit(solution)/shard_map/gather | solution.py:96
  625.4 5.9 bitcast_reduce_fusion
  (69 shorter events, 33.9 us)
Async XLA Ops:
  7.2 231.3 %copy-start = (bf16[1,2048,512]{2,1,0:T(8,128)(2,1)S(1)}, bf16[1,2048,512]{2,1,0:T(8,128)(2,1)}, u32[]{:S(2)}) copy-start(bf16[1,2048,512]{2,1,0:T(8,128)(2,1)} %param.11) | copy-start | bytes 6291460
  28.8 27.2 %copy-start.4 = (bf16[128,2048]{1,0:T(8,128)(2,1)S(1)}, bf16[128,2048]{1,0:T(8,128)(2,1)}, u32[]{:S(2)}) copy-start(bf16[128,2048]{1,0:T(8,128)(2,1)} %param.7) | copy-start | bytes 1572868
  40.9 28.7 %all-to-all-start = ((bf16[64,1,17]{2,1,0:T(2,128)(2,1)}), bf16[64,1,17]{2,1,0:T(2,128)(2,1)S(1)}, u32[]{:S(2)}, u32[]{:S(2)}) async-start(bf16[64,1,17]{2,1,0:T(2,128)(2,1)} %all_to_all.25), calls=%async_computation | async-start | bytes 65536 | tf_op jit(solution)/shard_map/all_to_all | solution.py:43
  69.6 12.6 %copy-start.5 = (bf16[128,2048]{1,0:T(8,128)(2,1)S(1)}, bf16[128,2048]{1,0:T(8,128)(2,1)}, u32[]{:S(2)}) copy-start(bf16[128,2048]{1,0:T(8,128)(2,1)} %param.8) | copy-start | bytes 1572868
  69.6 149.1 %all-to-all-start.2 = ((bf16[64,17,2048]{2,1,0:T(8,128)(2,1)}), bf16[64,17,2048]{2,1,0:T(8,128)(2,1)}, u32[]{:S(2)}, u32[]{:S(2)}) async-start(bf16[64,17,2048]{2,1,0:T(8,128)(2,1)} %reshape.121), calls=%async_computation.2 | async-start | bytes 12582912 | tf_op jit(solution)/shard_map/all_to_all | solution.py:42
  218.7 159.9 %all-to-all-start.1 = ((bf16[64,17,2048]{2,1,0:T(8,128)(2,1)}), bf16[64,17,2048]{2,1,0:T(8,128)(2,1)}, u32[]{:S(2)}, u32[]{:S(2)}) async-start(bf16[64,17,2048]{2,1,0:T(8,128)(2,1)} %reshape.119), calls=%async_computation.1 | async-start | bytes 12582912 | tf_op jit(solution)/shard_map/all_to_all | solution.py:54
  230.2 401.1 %reduce-scatter.8.cloned.1.call-start = ((), (), s32[]{:S(2)}) async-start(), calls=%async_computation.10 | async-start | bytes 2621440 | tf_op jit(solution)/shard_map/reduce_scatter | solution.py:92
  238.5 6.2 copy-start.2
  238.5 6.2 copy-start.6
  386.3 9.2 %copy-start.3 = (bf16[1088,2048]{1,0:T(8,128)(2,1)S(1)}, bf16[1088,2048]{1,0:T(8,128)(2,1)}, u32[]{:S(2)}) copy-start(bf16[1088,2048]{1,0:T(8,128)(2,1)} %reshape.120) | copy-start | bytes 13369348
  400.8 22.0 %all-to-all-start.4 = ((bf16[64,1,17]{2,1,0:T(2,128)(2,1)}), bf16[64,1,17]{2,1,0:T(2,128)(2,1)S(1)}, u32[]{:S(2)}, u32[]{:S(2)}) async-start(bf16[64,1,17]{2,1,0:T(2,128)(2,1)} %convert_element_type.87), calls=%async_computation.4 | async-start | bytes 65536 | tf_op jit(solution)/shard_map/all_to_all | solution.py:77
  406.6 3.9 copy-start.7
  406.6 3.9 copy-start.9
  422.7 183.1 %all-to-all-start.3 = ((bf16[64,17,2048]{2,1,0:T(8,128)(2,1)}), bf16[64,17,2048]{2,1,0:T(8,128)(2,1)}, u32[]{:S(2)}, u32[]{:S(2)}) async-start(bf16[64,17,2048]{2,1,0:T(8,128)(2,1)} %reshape.123), calls=%async_computation.3 | async-start | bytes 12582912 | tf_op jit(solution)/shard_map/all_to_all | solution.py:70
  435.0 7.3 %copy-start.8 = (bf16[1088,512]{1,0:T(8,128)(2,1)S(1)}, bf16[1088,512]{1,0:T(8,128)(2,1)}, u32[]{:S(2)}) copy-start(bf16[1088,512]{1,0:T(8,128)(2,1)} %get-tuple-element.17) | copy-start | bytes 3342340
  435.0 196.3 %reduce-scatter.6.cloned.1.call-start = ((), (), s32[]{:S(2)}) async-start(), calls=%async_computation.9 | async-start | bytes 2621440 | tf_op jit(solution)/shard_map/reduce_scatter | solution.py:89
  442.0 189.3 %reduce-scatter.4.cloned.1.call-start = ((), (), s32[]{:S(2)}) async-start(), calls=%async_computation.8 | async-start | bytes 2621440 | tf_op jit(solution)/shard_map/reduce_scatter | solution.py:86
  613.6 17.7 %copy-start.1 = (bf16[1,2048,512]{2,1,0:T(8,128)(2,1)S(1)}, bf16[1,2048,512]{2,1,0:T(8,128)(2,1)}, u32[]{:S(2)}) copy-start(bf16[1,2048,512]{2,1,0:T(8,128)(2,1)} %param.11) | copy-start | bytes 6291460
Sparse Core Ops, SparseCore 0:
  400.1 25.7 reduce-scatter.7
  442.1 87.7 reduce-scatter.5
  533.1 62.0 reduce-scatter.3
where the time goes:
time: 641 us; the launch traced here: 638 us
  waiting for transfers between devices  402 us (63%)
  local copies, waits for them, and re-layouts  92.9 us (14%)
  starting transfers between devices  57.8 us (9%)
  matrix products  45.7 us (7%)
  other arithmetic  25.2 us (4%)
  between operations  14.1 us (2%)
    all_to_all x1, waiting for transfers between devices, shards(): lax.all_to_all(d_rows.reshape(experts, capacity, model_width), 'expert',...  149 us
    all_to_all x1, waiting for transfers between devices, shards(): lax.all_to_all(dy_send, 'expert', split_axis=0, concat_axis=0, tiled=True)  130 us
    all_to_all x1, waiting for transfers between devices, shards(): lax.all_to_all(x_send, 'expert', split_axis=0, concat_axis=0, tiled=True)  123 us
    dot_general x6, matrix products, contract(): lax.dot_general(left, right, (((left_dim,), (right_dim,)), ((), ())), pre...  35.6 us
    another operation x3, other arithmetic  18.2 us
    all_to_all x1, starting transfers between devices, shards(): lax.all_to_all(p_send, 'expert', split_axis=0, concat_axis=0, tiled=True)  15.1 us
  transfers between devices with their start and end apart: 8, of which 3 were waited for; matrix products, arithmetic and copies ran while one was open for 17% of the time, Pallas kernels for 0%

commit v1 on v0

v1 whole, which is shorter than its diff:
```python
import jax
import jax.numpy as jnp
from jax import lax
from jax.experimental import pallas as pl
from jax.experimental.pallas import tpu as pltpu
from jax.sharding import PartitionSpec as P

MESH = pl.DeviceIdType.MESH
BF, F32 = jnp.bfloat16, jnp.float32

D = 2048
F = 512
T = 128
TOP = 8
NP = 16
NZ = 8
SLOTS = 16
MAIN = NP * SLOTS
ROWS = MAIN + NP
LANE = 128
WIDE = D + LANE
BACK = WIDE + LANE
NCH = 4
OTHERS = MAIN - SLOTS
QD = D // 4


def dot(left, right, left_dim=1, right_dim=0):
    return lax.dot_general(
        left, right, (((left_dim,), (right_dim,)), ((), ())), preferred_element_type=F32
    )


def iota(shape, dim):
    return lax.broadcasted_iota(jnp.int32, shape, dim)


def kernel(
    tok_hbm, dout_hbm, prob_ref, routes_ref, wg_hbm, wu_hbm, wd_hbm,
    dtok_ref, dprob_ref, gout_ref,
    zl_ref, meta_all, meta, onehot, perm, expand, snd, rxz, wts, rows_x, rows_z, extra,
    dall, rrcv, zsnd, zrcv, acc, core_rcv, low_rcv,
    load_sem, zs_sem, zr_sem, ms_sem, mr_sem, as_sem, ar_sem, bs_sem, br_sem,
    ts_sem, tr_sem, cs_sem, cr_sem, ls_sem, lr_sem,
):
    dp, ex = lax.axis_index("dp"), lax.axis_index("expert")
    core, low = lax.rem(dp, 2), lax.div(dp, 2)
    high, me = lax.rem(ex, 4), lax.div(ex, 4)
    z = high * 2 + low
    sign = 1 - 2 * low

    def column(offset):
        there = lax.rem(z + offset + 2 * NZ, NZ)
        return (lax.rem(there, 2) * 2 + core, me * 4 + lax.div(there, 2))

    def plane(number):
        return (dp, number * 4 + high)

    other_core = (low * 2 + 1 - core, ex)
    other_low = ((1 - low) * 2 + core, ex)

    def remote(src, dst, send, recv, device):
        return pltpu.make_async_remote_copy(
            src_ref=src, dst_ref=dst, send_sem=send, recv_sem=recv,
            device_id=device, device_id_type=MESH,
        )

    def wait_for(ref, sem):
        pltpu.make_async_copy(ref, ref, sem).wait()

    loads = [
        pltpu.make_async_copy(tok_hbm, zl_ref.at[0, 0], load_sem.at[0]),
        pltpu.make_async_copy(dout_hbm, zl_ref.at[1, 0], load_sem.at[1]),
        pltpu.make_async_copy(wg_hbm, wts.at[0], load_sem.at[2]),
        pltpu.make_async_copy(wu_hbm, wts.at[1], load_sem.at[3]),
    ] + [
        pltpu.make_async_copy(wd_hbm.at[:, QD * r : QD * (r + 1)], wts.at[2, r], load_sem.at[4 + r])
        for r in range(4)
    ]
    for load in loads:
        load.start()

    barrier = pltpu.get_barrier_semaphore()

    def greet(device):
        pl.semaphore_signal(barrier, inc=1, device_id=device, device_id_type=MESH)

    def greet_plane(step, carry):
        greet(plane(lax.rem(me + step, NP)))
        return carry

    lax.fori_loop(1, NP, greet_plane, 0)
    for offset in (-sign, -3 * sign, 2 * sign, -2 * sign):
        greet(column(offset))
    greet(other_core)
    greet(other_low)
    pl.semaphore_wait(barrier, NP - 1 + 6)

    for a in range(2):
        loads[a].wait()
        remote(
            zl_ref.at[a, 0], zl_ref.at[a, 1], zs_sem.at[a, 0], zr_sem.at[a, 0], column(-sign)
        ).start()

    routes = routes_ref[...]
    rank = (routes & 3) * NP + (routes >> 2)
    probs = prob_ref[...].astype(F32)
    lane = iota((T, LANE), 1)
    named = jnp.zeros((T, LANE), F32)
    weight = jnp.zeros((T, LANE), F32)
    for k in range(TOP):
        hit = rank[:, k : k + 1] == lane
        named = named + jnp.where(hit, 1.0, 0.0)
        weight = weight + jnp.where(hit, probs[:, k : k + 1], 0.0)
    earlier = jnp.where(iota((T, T), 1) < iota((T, T), 0), 1.0, 0.0).astype(BF)
    slot = dot(earlier, named.astype(BF))
    slot = jnp.where(named > 0.5, slot, -1.0).T
    weight = weight.T
    for h in range(4):
        meta_all[32 * h : 32 * h + 16, :] = slot[16 * h : 16 * h + 16].astype(BF)
        meta_all[32 * h + 16 : 32 * h + 32, :] = weight[16 * h : 16 * h + 16].astype(BF)
    for j, offset in enumerate((-sign, 2 * sign, -3 * sign)):
        there = lax.div(lax.rem(z + offset + 2 * NZ, NZ), 2)
        remote(
            meta_all.at[pl.ds(pl.multiple_of(there * 32, 32), 32), :],
            meta.at[j + 1], ms_sem.at[j], mr_sem.at[j], column(offset),
        ).start()
    meta[0] = meta_all[pl.ds(pl.multiple_of(high * 32, 32), 32), :]

    row, col = iota((MAIN, MAIN), 0), iota((MAIN, MAIN), 1)
    perm[...] = jnp.where(col == (row & 15) * 16 + (row >> 4), 1.0, 0.0).astype(BF)
    expand[...] = jnp.where(iota((MAIN, NP), 0) >> 4 == iota((MAIN, NP), 1), 1.0, 0.0).astype(BF)

    def to_tiles(value):
        stacked = jnp.concatenate([value[:, LANE * j : LANE * (j + 1)] for j in range(16)], axis=0)
        return dot(perm[...], stacked).astype(BF)

    def from_tiles(tiles):
        stacked = dot(perm[...], tiles).astype(BF)
        return [stacked[16 * j : 16 * j + 16] for j in range(16)]

    def dispatch(c):
        @pl.when(c >= 1)
        def _():
            wait_for(meta.at[c], mr_sem.at[c - 1])

        slots, weights = meta[c, 0:16, :], meta[c, 16:32, :]
        at_slot = dot(expand[...], slots) == (iota((MAIN, T), 0) & 15).astype(F32)
        last = slots.astype(F32) == float(SLOTS)
        onehot[c, 0, 0:MAIN, :] = jnp.where(at_slot, 1.0, 0.0).astype(BF)
        onehot[c, 0, MAIN:ROWS, :] = jnp.where(last, 1.0, 0.0).astype(BF)
        onehot[c, 1, 0:MAIN, :] = jnp.where(at_slot, dot(expand[...], weights), 0.0).astype(BF)
        onehot[c, 1, MAIN:ROWS, :] = jnp.where(last, weights.astype(F32), 0.0).astype(BF)

        for a in range(2):
            @pl.when(c >= 1)
            def _():
                wait_for(zl_ref.at[a, c], zr_sem.at[a, c - 1])

            @pl.when(c == 1)
            def _():
                remote(
                    zl_ref.at[a, 0], zl_ref.at[a, 2], zs_sem.at[a, 1], zr_sem.at[a, 1],
                    column(2 * sign),
                ).start()

            @pl.when(c == 2)
            def _():
                remote(
                    zl_ref.at[a, 1], zl_ref.at[a, 3], zs_sem.at[a, 2], zr_sem.at[a, 2],
                    column(2 * sign),
                ).start()

            tail = []
            for r in range(4):
                packed = dot(onehot[c, a], zl_ref[a, c, :, QD * r : QD * (r + 1)]).astype(BF)
                snd[a, c, :, QD * r : QD * (r + 1)] = packed[0:MAIN]
                tail.append(packed[MAIN:ROWS])
            snd[a, c, :, D:WIDE] = to_tiles(jnp.concatenate(tail, axis=1))

            mine = pl.ds(pl.multiple_of(me * SLOTS, SLOTS), SLOTS)

            def send(step, carry):
                to = lax.rem(me + step, NP)
                remote(
                    snd.at[a, c, pl.ds(pl.multiple_of(to * SLOTS, SLOTS), SLOTS), 0:WIDE],
                    rxz.at[a, c, mine, :], as_sem.at[a, c], ar_sem.at[a, c], plane(to),
                ).start()
                return carry

            lax.fori_loop(1, NP, send, 0)
            rxz[a, c, mine, :] = snd[a, c, mine, 0:WIDE]

    def expert(c):
        here = pl.ds(pl.multiple_of(c * MAIN, MAIN), MAIN)
        spare = pl.ds(pl.multiple_of(NCH * MAIN + c * NP, NP), NP)
        side = pl.ds(pl.multiple_of(c * NP, NP), NP)
        for a, rows in ((0, rows_x), (1, rows_z)):
            wait_for(rxz.at[a, c, 0:OTHERS, :], ar_sem.at[a, c])
            rows[0:MAIN, 0:D] = rxz[a, c, :, 0:D]
            for j, block in enumerate(from_tiles(rxz[a, c, :, D:WIDE])):
                rows[MAIN:ROWS, LANE * j : LANE * (j + 1)] = block
                extra[a, side, LANE * j : LANE * (j + 1)] = block
        gate = dot(rows_x[:, 0:QD], wts[0, 0])
        up = dot(rows_x[:, 0:QD], wts[1, 0])
        back = dot(rows_z[:, 0:QD], wts[2, 0], 1, 1)
        for r in range(1, 4):
            part = slice(QD * r, QD * (r + 1))
            gate = gate + dot(rows_x[:, part], wts[0, r])
            up = up + dot(rows_x[:, part], wts[1, r])
            back = back + dot(rows_z[:, part], wts[2, r], 1, 1)
        sig = jax.nn.sigmoid(gate)
        silu = gate * sig
        hidden = (silu * up).astype(BF)
        prob = jnp.sum(hidden.astype(F32) * back, axis=1, keepdims=True)
        d_gate = (back * up * sig * (1.0 + gate * (1.0 - sig))).astype(BF)
        d_up = (back * silu).astype(BF)
        for g, value in ((0, d_gate), (1, d_up), (2, hidden)):
            dall[g, here, :] = value[0:MAIN]
            dall[g, spare, :] = value[MAIN:ROWS]
        wait_for(snd.at[0, c, 0:OTHERS, 0:WIDE], as_sem.at[0, c])
        tail = []
        for r in range(4):
            d_rows = (dot(d_gate, wts[0, r], 1, 1) + dot(d_up, wts[1, r], 1, 1)).astype(BF)
            snd[0, c, :, QD * r : QD * (r + 1)] = d_rows[0:MAIN]
            tail.append(d_rows[MAIN:ROWS])
        snd[0, c, :, D:WIDE] = to_tiles(jnp.concatenate(tail, axis=1))
        prob_main = jnp.broadcast_to(prob[0:MAIN], (MAIN, LANE))
        prob_last = dot(expand[...], jnp.broadcast_to(prob[MAIN:ROWS], (NP, LANE)).astype(BF))
        snd[0, c, :, WIDE:BACK] = jnp.where(
            iota((MAIN, LANE), 1) < 64, prob_main, prob_last
        ).astype(BF)

        mine = pl.ds(pl.multiple_of(me * SLOTS, SLOTS), SLOTS)

        def send(step, carry):
            to = lax.rem(me + step, NP)
            remote(
                snd.at[0, c, pl.ds(pl.multiple_of(to * SLOTS, SLOTS), SLOTS), :],
                rrcv.at[c, mine, :], bs_sem.at[c], br_sem.at[c], plane(to),
            ).start()
            return carry

        lax.fori_loop(1, NP, send, 0)
        rrcv[c, mine, :] = snd[0, c, mine, :]

    def combine(c):
        wait_for(rrcv.at[c, 0:OTHERS, :], br_sem.at[c])
        rows_x[0:MAIN, 0:D] = rrcv[c, :, 0:D]
        for j, block in enumerate(from_tiles(rrcv[c, :, D:WIDE])):
            rows_x[MAIN:ROWS, LANE * j : LANE * (j + 1)] = block
        tile = rrcv[c, :, WIDE:BACK]
        owner = iota((MAIN, LANE), 0) >> 4
        rows_x[0:MAIN, D:WIDE] = jnp.where(
            iota((MAIN, LANE), 1) == owner + high * NP, tile.astype(F32), 0.0
        ).astype(BF)
        first = jnp.where(iota((NP, MAIN), 1) == iota((NP, MAIN), 0) * SLOTS, 1.0, 0.0).astype(BF)
        rows_x[MAIN:ROWS, D:WIDE] = jnp.where(
            iota((NP, LANE), 1) == iota((NP, LANE), 0) + high * NP + 64, dot(first, tile), 0.0
        ).astype(BF)
        return dot(onehot[c, 0], rows_x[...], 0, 0)

    def combine_far(c):
        zsnd[c - 1] = combine(c).astype(BF)
        remote(
            zsnd.at[c - 1], zrcv.at[c - 1], ts_sem.at[c - 1], tr_sem.at[c - 1], column(-c * sign)
        ).start()

    dispatch(0)
    for load in loads[2:]:
        load.wait()

    def step(c, carry):
        @pl.when(c < NCH - 1)
        def _():
            dispatch(c + 1)

        expert(c)

        @pl.when(c >= 2)
        def _():
            combine_far(c - 1)

        return carry

    lax.fori_loop(0, NCH, step, 0)

    def weight_gradient(g, r):
        a = lax.div(g, 2)
        part = pl.ds(pl.multiple_of(r * QD, QD), QD)
        main = dall[g, 0 : NCH * MAIN, :]
        total = dot(main, rxz[a, :, :, part].reshape(NCH * MAIN, QD), 0, 0)
        total = total + dot(dall[g, NCH * MAIN : NCH * ROWS, :], extra[a, :, part], 0, 0)
        wts[g, r] = total.astype(BF)

    def to_core(i, carry):
        g, half = lax.div(i, 2), lax.rem(i, 2)
        r = half * 2 + 1 - core
        weight_gradient(g, r)
        remote(
            wts.at[g, r], core_rcv.at[g, half], cs_sem.at[g, half], cr_sem.at[g, half], other_core
        ).start()
        return carry

    lax.fori_loop(0, 6, to_core, 0)

    def to_low(g, carry):
        r = (1 - low) * 2 + core
        weight_gradient(g, r)
        wait_for(core_rcv.at[g, 1 - low], cr_sem.at[g, 1 - low])
        wts[g, r] = (wts[g, r].astype(F32) + core_rcv[g, 1 - low].astype(F32)).astype(BF)
        remote(wts.at[g, r], low_rcv.at[g], ls_sem.at[g], lr_sem.at[g], other_low).start()
        return carry

    lax.fori_loop(0, 3, to_low, 0)
    combine_far(NCH - 1)

    def to_own(g, carry):
        weight_gradient(g, low * 2 + core)
        return carry

    lax.fori_loop(0, 3, to_own, 0)
    acc[...] = combine(0)

    def finish(g, carry):
        r = low * 2 + core
        wait_for(core_rcv.at[g, low], cr_sem.at[g, low])
        wait_for(low_rcv.at[g], lr_sem.at[g])
        gout_ref[g] = (
            wts[g, r].astype(F32) + core_rcv[g, low].astype(F32) + low_rcv[g].astype(F32)
        ).astype(BF)
        return carry

    lax.fori_loop(0, 3, finish, 0)
    for j in range(NCH - 1):
        wait_for(zrcv.at[j], tr_sem.at[j])
    total = acc[...]
    for j in range(NCH - 1):
        total = total + zrcv[j].astype(F32)
    dtok_ref[...] = total[:, 0:D].astype(BF)
    entries = total[:, D:WIDE]
    d_probs = jnp.zeros((T, TOP), F32)
    for k in range(TOP):
        entry = jnp.sum(
            jnp.where((lane & 63) == rank[:, k : k + 1], entries, 0.0), axis=1, keepdims=True
        )
        d_probs = d_probs + jnp.where(iota((T, TOP), 1) == k, entry, 0.0)
    dprob_ref[...] = (d_probs / probs).astype(BF)

    for j in range(NCH - 1):
        for a in range(2):
            wait_for(zl_ref.at[a, 0], zs_sem.at[a, j])
        wait_for(meta.at[0], ms_sem.at[j])
        wait_for(zsnd.at[j], ts_sem.at[j])
    for c in range(NCH):
        wait_for(snd.at[1, c, 0:OTHERS, 0:WIDE], as_sem.at[1, c])
        wait_for(snd.at[0, c, 0:OTHERS, :], bs_sem.at[c])
    for g in range(3):
        for half in range(2):
            wait_for(core_rcv.at[g, half], cs_sem.at[g, half])
        wait_for(low_rcv.at[g], ls_sem.at[g])


def shards(tokens, d_out, route_probs, routes, w_gate, w_up, w_down):
    dma = pltpu.SemaphoreType.DMA
    anywhere, vmem = pl.BlockSpec(memory_space=pl.ANY), pl.BlockSpec(memory_space=pltpu.VMEM)
    d_tokens, d_probs, grads = pl.pallas_call(
        kernel,
        out_shape=(
            jax.ShapeDtypeStruct((T, D), BF),
            jax.ShapeDtypeStruct((T, TOP), BF),
            jax.ShapeDtypeStruct((3, F, QD), BF),
        ),
        in_specs=[anywhere, anywhere, vmem, vmem, anywhere, anywhere, anywhere],
        out_specs=(vmem, vmem, vmem),
        scratch_shapes=[
            pltpu.VMEM((2, NCH, T, D), BF),
            pltpu.VMEM((T, LANE), BF),
            pltpu.VMEM((NCH, 32, LANE), BF),
            pltpu.VMEM((NCH, 2, ROWS, T), BF),
            pltpu.VMEM((MAIN, MAIN), BF),
            pltpu.VMEM((MAIN, NP), BF),
            pltpu.VMEM((2, NCH, MAIN, BACK), BF),
            pltpu.VMEM((2, NCH, MAIN, WIDE), BF),
            pltpu.VMEM((3, 4, F, QD), BF),
            pltpu.VMEM((ROWS, WIDE), BF),
            pltpu.VMEM((ROWS, D), BF),
            pltpu.VMEM((2, NCH * NP, D), BF),
            pltpu.VMEM((3, NCH * ROWS, F), BF),
            pltpu.VMEM((NCH, MAIN, BACK), BF),
            pltpu.VMEM((NCH - 1, T, WIDE), BF),
            pltpu.VMEM((NCH - 1, T, WIDE), BF),
            pltpu.VMEM((T, WIDE), F32),
            pltpu.VMEM((3, 2, F, QD), BF),
            pltpu.VMEM((3, F, QD), BF),
            dma((8,)),
            dma((2, 3)), dma((2, 3)), dma((3,)), dma((3,)),
            dma((2, NCH)), dma((2, NCH)), dma((NCH,)), dma((NCH,)),
            dma((3,)), dma((3,)), dma((3, 2)), dma((3, 2)), dma((3,)), dma((3,)),
        ],
        compiler_params=pltpu.CompilerParams(
            collective_id=0, has_side_effects=True, vmem_limit_bytes=62 << 20
        ),
    )(
        tokens, d_out, route_probs, routes,
        w_gate.reshape(4, QD, F), w_up.reshape(4, QD, F), w_down.reshape(F, D),
    )
    return (
        d_tokens,
        d_probs,
        grads[0].T[None],
        grads[1].T[None],
        grads[2][None],
    )


def solution(mesh):
    return jax.shard_map(
        shards,
        mesh=mesh,
        in_specs=(
            P(("dp", "expert"), None),
            P(("dp", "expert"), None),
            P(("dp", "expert"), None),
            P(("dp", "expert"), None),
            P("expert", None, None),
            P("expert", None, None),
            P("expert", None, None),
        ),
        out_specs=(
            P(("dp", "expert"), None),
            P(("dp", "expert"), None),
            P("expert", "dp", None),
            P("expert", "dp", None),
            P("expert", None, "dp"),
        ),
        check_vma=False,
    )
```

time: 641 us -> 249 us (0.39)
  the two profiles are of different devices: /device:TPU:1 before, /device:TPU:252 now
where the time goes in v1:
time: 249 us; the launch traced here: 248 us
  Pallas kernels  238 us (96%)
  local copies, waits for them, and re-layouts  9.33 us (4%)
    pallas_call x1, Pallas kernels, shards(): pl.pallas_call(kernel, out_shape=(jax.ShapeDtypeStruct((T, D), BF), jax.S...  238 us
    unnamed x8, local copies, waits for them, and re-layouts  7.02 us

profile of v1, /device:TPU:252, one launch (start us, length us, event | category | flops | bytes accessed | tf_op | source)
XLA Modules:
  0.0 248.3 jit_solution(13104982160301449945)
XLA Ops:
  0.6 1.4 copy.12.prob_ref
  2.0 1.4 copy.13.routes_ref
  3.4 238.3 %shard_map.110 = (bf16[128,2048]{1,0:T(8,128)(2,1)}, bf16[128,8]{1,0:T(8,128)(2,1)}, bf16[3,512,512]{2,1,0:T(8,128)(2,1)}) custom-call(bf16[128,2048]{1,0:T(8,128)(2,1)} %tok_hbm.1, bf16[128,2048]{1,0:T(8,128)(2,1)} %dout_hbm.1, bf16[128,8]{1,0:T(8,128)(2,1)} %copy.12.prob_ref, s32[128,8]{1,0:T(8,128)} %copy.13.routes_ref, bf16[4,512,512]{2,1,0:T(8,128)(2,1)} %bitcast.15, ...), custom_call_target="tpu_custom_call" | custom-call | tf_op jit(solution)/shard_map/pallas_call | solution.py:367
  241.8 1.4 copy.14
  243.2 0.0 copy-start
  243.2 2.3 fusion
  245.5 1.0 copy.16
  246.5 1.0 copy.15
  247.5 0.0 copy-done
  247.5 0.8 copy.18
Async XLA Ops:
  243.2 4.3 %copy-start = (bf16[128,2048]{1,0:T(8,128)(2,1)S(1)}, bf16[128,2048]{1,0:T(8,128)(2,1)}, u32[]{:S(2)}) copy-start(bf16[128,2048]{1,0:T(8,128)(2,1)} %get-tuple-element.24) | copy-start | bytes 1572868

commit v2 on v1

--- a/solution.py
+++ b/solution.py
@@ -37,7 +37,7 @@
 
 def kernel(
     tok_hbm, dout_hbm, prob_ref, routes_ref, wg_hbm, wu_hbm, wd_hbm,
-    dtok_ref, dprob_ref, gout_ref,
+    dtok_ref, dprob_ref, ggate_ref, gup_ref, gdown_ref,
     zl_ref, meta_all, meta, onehot, perm, expand, snd, rxz, wts, rows_x, rows_z, extra,
     dall, rrcv, zsnd, zrcv, acc, core_rcv, low_rcv,
     load_sem, zs_sem, zr_sem, ms_sem, mr_sem, as_sem, ar_sem, bs_sem, br_sem,
@@ -52,6 +52,10 @@
     def column(offset):
         there = lax.rem(z + offset + 2 * NZ, NZ)
         return (lax.rem(there, 2) * 2 + core, me * 4 + lax.div(there, 2))
+
+    def around(step):
+        there_x = lax.rem(lax.div(me, 4) + lax.div(step, 4), 4)
+        return there_x * 4 + lax.rem(lax.rem(me, 4) + lax.rem(step, 4), 4)
 
     def plane(number):
         return (dp, number * 4 + high)
@@ -96,26 +100,28 @@
     greet(other_low)
     pl.semaphore_wait(barrier, NP - 1 + 6)
 
-    for a in range(2):
-        loads[a].wait()
+    def along_z(c, a):
         remote(
-            zl_ref.at[a, 0], zl_ref.at[a, 1], zs_sem.at[a, 0], zr_sem.at[a, 0], column(-sign)
+            zl_ref.at[a, jnp.where(c == 3, 1, 0)], zl_ref.at[a, c],
+            zs_sem.at[a, c - 1], zr_sem.at[a, c - 1], column(jnp.where(c == 1, -sign, 2 * sign)),
         ).start()
+
+    loads[0].wait()
+    along_z(1, 0)
+    loads[1].wait()
 
     routes = routes_ref[...]
     rank = (routes & 3) * NP + (routes >> 2)
     probs = prob_ref[...].astype(F32)
-    lane = iota((T, LANE), 1)
-    named = jnp.zeros((T, LANE), F32)
-    weight = jnp.zeros((T, LANE), F32)
+    number = iota((64, T), 0)
+    named = jnp.zeros((64, T), F32)
+    weight = jnp.zeros((64, T), F32)
     for k in range(TOP):
-        hit = rank[:, k : k + 1] == lane
+        hit = rank[k : k + 1, :] == number
         named = named + jnp.where(hit, 1.0, 0.0)
-        weight = weight + jnp.where(hit, probs[:, k : k + 1], 0.0)
-    earlier = jnp.where(iota((T, T), 1) < iota((T, T), 0), 1.0, 0.0).astype(BF)
-    slot = dot(earlier, named.astype(BF))
-    slot = jnp.where(named > 0.5, slot, -1.0).T
-    weight = weight.T
+        weight = weight + jnp.where(hit, probs[k : k + 1, :], 0.0)
+    earlier = jnp.where(iota((T, T), 0) < iota((T, T), 1), 1.0, 0.0).astype(BF)
+    slot = jnp.where(named > 0.5, dot(named.astype(BF), earlier), -1.0)
     for h in range(4):
         meta_all[32 * h : 32 * h + 16, :] = slot[16 * h : 16 * h + 16].astype(BF)
         meta_all[32 * h + 16 : 32 * h + 32, :] = weight[16 * h : 16 * h + 16].astype(BF)
@@ -152,24 +158,14 @@
         onehot[c, 1, 0:MAIN, :] = jnp.where(at_slot, dot(expand[...], weights), 0.0).astype(BF)
         onehot[c, 1, MAIN:ROWS, :] = jnp.where(last, weights.astype(F32), 0.0).astype(BF)
 
-        for a in range(2):
+        def one(a, carry):
             @pl.when(c >= 1)
             def _():
                 wait_for(zl_ref.at[a, c], zr_sem.at[a, c - 1])
 
-            @pl.when(c == 1)
+            @pl.when((c >= 1) & (2 * c + a < 7))
             def _():
-                remote(
-                    zl_ref.at[a, 0], zl_ref.at[a, 2], zs_sem.at[a, 1], zr_sem.at[a, 1],
-                    column(2 * sign),
-                ).start()
-
-            @pl.when(c == 2)
-            def _():
-                remote(
-                    zl_ref.at[a, 1], zl_ref.at[a, 3], zs_sem.at[a, 2], zr_sem.at[a, 2],
-                    column(2 * sign),
-                ).start()
+                along_z(c + a, 1 - a)
 
             tail = []
             for r in range(4):
@@ -181,7 +177,7 @@
             mine = pl.ds(pl.multiple_of(me * SLOTS, SLOTS), SLOTS)
 
             def send(step, carry):
-                to = lax.rem(me + step, NP)
+                to = around(step)
                 remote(
                     snd.at[a, c, pl.ds(pl.multiple_of(to * SLOTS, SLOTS), SLOTS), 0:WIDE],
                     rxz.at[a, c, mine, :], as_sem.at[a, c], ar_sem.at[a, c], plane(to),
@@ -190,6 +186,9 @@
 
             lax.fori_loop(1, NP, send, 0)
             rxz[a, c, mine, :] = snd[a, c, mine, 0:WIDE]
+            return carry
+
+        lax.fori_loop(0, 2, one, 0)
 
     def expert(c):
         here = pl.ds(pl.multiple_of(c * MAIN, MAIN), MAIN)
@@ -231,10 +230,11 @@
             iota((MAIN, LANE), 1) < 64, prob_main, prob_last
         ).astype(BF)
 
+    def give_back(c):
         mine = pl.ds(pl.multiple_of(me * SLOTS, SLOTS), SLOTS)
 
         def send(step, carry):
-            to = lax.rem(me + step, NP)
+            to = around(step)
             remote(
                 snd.at[0, c, pl.ds(pl.multiple_of(to * SLOTS, SLOTS), SLOTS), :],
                 rrcv.at[c, mine, :], bs_sem.at[c], br_sem.at[c], plane(to),
@@ -275,15 +275,17 @@
         def _():
             dispatch(c + 1)
 
+        @pl.when(c == NCH - 2)
+        def _():
+            give_back(1)
+
         expert(c)
 
-        @pl.when(c >= 2)
-        def _():
-            combine_far(c - 1)
-
         return carry
 
     lax.fori_loop(0, NCH, step, 0)
+    for c in (3, 2, 0):
+        give_back(c)
 
     def weight_gradient(g, r):
         a = lax.div(g, 2)
@@ -313,38 +315,40 @@
         return carry
 
     lax.fori_loop(0, 3, to_low, 0)
-    combine_far(NCH - 1)
+    combine_far(1)
 
     def to_own(g, carry):
         weight_gradient(g, low * 2 + core)
         return carry
 
     lax.fori_loop(0, 3, to_own, 0)
+    combine_far(3)
+    combine_far(2)
     acc[...] = combine(0)
 
-    def finish(g, carry):
-        r = low * 2 + core
+    def finish(g):
         wait_for(core_rcv.at[g, low], cr_sem.at[g, low])
         wait_for(low_rcv.at[g], lr_sem.at[g])
-        gout_ref[g] = (
-            wts[g, r].astype(F32) + core_rcv[g, low].astype(F32) + low_rcv[g].astype(F32)
-        ).astype(BF)
-        return carry
-
-    lax.fori_loop(0, 3, finish, 0)
+        own = wts[g, low * 2 + core].astype(F32)
+        return own + core_rcv[g, low].astype(F32) + low_rcv[g].astype(F32)
+
+    ggate_ref[...] = finish(0).T.astype(BF)
+    gup_ref[...] = finish(1).T.astype(BF)
+    gdown_ref[...] = finish(2).astype(BF)
     for j in range(NCH - 1):
         wait_for(zrcv.at[j], tr_sem.at[j])
     total = acc[...]
     for j in range(NCH - 1):
         total = total + zrcv[j].astype(F32)
     dtok_ref[...] = total[:, 0:D].astype(BF)
-    entries = total[:, D:WIDE]
-    d_probs = jnp.zeros((T, TOP), F32)
+    entries = total[:, D:WIDE].T
+    entries = entries[0:64] + entries[64:LANE]
+    d_probs = jnp.zeros((TOP, T), F32)
     for k in range(TOP):
         entry = jnp.sum(
-            jnp.where((lane & 63) == rank[:, k : k + 1], entries, 0.0), axis=1, keepdims=True
+            jnp.where(number == rank[k : k + 1, :], entries, 0.0), axis=0, keepdims=True
         )
-        d_probs = d_probs + jnp.where(iota((T, TOP), 1) == k, entry, 0.0)
+        d_probs = d_probs + jnp.where(iota((TOP, T), 0) == k, entry, 0.0)
     dprob_ref[...] = (d_probs / probs).astype(BF)
 
     for j in range(NCH - 1):
@@ -364,15 +368,17 @@
 def shards(tokens, d_out, route_probs, routes, w_gate, w_up, w_down):
     dma = pltpu.SemaphoreType.DMA
     anywhere, vmem = pl.BlockSpec(memory_space=pl.ANY), pl.BlockSpec(memory_space=pltpu.VMEM)
-    d_tokens, d_probs, grads = pl.pallas_call(
+    d_tokens, d_probs, g_gate, g_up, g_down = pl.pallas_call(
         kernel,
         out_shape=(
             jax.ShapeDtypeStruct((T, D), BF),
-            jax.ShapeDtypeStruct((T, TOP), BF),
-            jax.ShapeDtypeStruct((3, F, QD), BF),
+            jax.ShapeDtypeStruct((TOP, T), BF),
+            jax.ShapeDtypeStruct((QD, F), BF),
+            jax.ShapeDtypeStruct((QD, F), BF),
+            jax.ShapeDtypeStruct((F, QD), BF),
         ),
         in_specs=[anywhere, anywhere, vmem, vmem, anywhere, anywhere, anywhere],
-        out_specs=(vmem, vmem, vmem),
+        out_specs=(vmem, vmem, vmem, vmem, vmem),
         scratch_shapes=[
             pltpu.VMEM((2, NCH, T, D), BF),
             pltpu.VMEM((T, LANE), BF),
@@ -402,15 +408,15 @@
             collective_id=0, has_side_effects=True, vmem_limit_bytes=62 << 20
         ),
     )(
-        tokens, d_out, route_probs, routes,
+        tokens, d_out, route_probs.T, routes.T,
         w_gate.reshape(4, QD, F), w_up.reshape(4, QD, F), w_down.reshape(F, D),
     )
     return (
         d_tokens,
-        d_probs,
-        grads[0].T[None],
-        grads[1].T[None],
-        grads[2][None],
+        d_probs.T,
+        g_gate[None],
+        g_up[None],
+        g_down[None],
     )
 
 

time: 249 us -> 201 us (0.81)
  the two profiles are of different devices: /device:TPU:252 before, /device:TPU:54 now
where the time goes in v2:
time: 201 us
  Pallas kernels  193 us (96%)
  local copies, waits for them, and re-layouts  6.68 us (3%)
    pallas_call x1, Pallas kernels, shards(): pl.pallas_call(kernel, out_shape=(jax.ShapeDtypeStruct((T, D), BF), jax.S...  193 us
    unnamed x9, local copies, waits for them, and re-layouts  6.68 us

profile of v2, /device:TPU:54, one launch (start us, length us, event | category | flops | bytes accessed | tf_op | source)
XLA Modules:
  0.0 200.8 jit_solution(11862487528166621786)
XLA Ops:
  0.6 193.4 %shard_map.110 = (bf16[128,2048]{1,0:T(8,128)(2,1)}, bf16[8,128]{1,0:T(8,128)(2,1)}, bf16[512,512]{1,0:T(8,128)(2,1)}, bf16[512,512]{1,0:T(8,128)(2,1)}, bf16[512,512]{1,0:T(8,128)(2,1)}) custom-call(bf16[128,2048]{1,0:T(8,128)(2,1)} %tok_hbm.1, bf16[128,2048]{1,0:T(8,128)(2,1)} %dout_hbm.1, bf16[8,128]{1,0:T(8,128)(2,1)} %bitcast.17, s32[8,128]{1,0:T(8,128)} %bitcast.15, ...), custom_call_target="tpu_custom_call" | custom-call | tf_op jit(solution)/shard_map/pallas_call | solution.py:371
  194.1 0.0 copy-start.1
  194.1 0.0 copy-start
  194.1 2.0 copy.17
  196.1 1.3 copy.18
  197.3 1.9 copy.19
  199.2 0.0 copy-done.1
  199.2 0.8 copy.20
  200.0 0.0 copy-done
  200.0 0.8 copy.21
Async XLA Ops:
  194.1 5.1 %copy-start.1 = (bf16[512,512]{1,0:T(8,128)(2,1)S(1)}, bf16[512,512]{1,0:T(8,128)(2,1)}, u32[]{:S(2)}) copy-start(bf16[512,512]{1,0:T(8,128)(2,1)} %get-tuple-element.13) | copy-start | bytes 1572868
  194.1 5.9 %copy-start = (bf16[512,512]{1,0:T(8,128)(2,1)S(1)}, bf16[512,512]{1,0:T(8,128)(2,1)}, u32[]{:S(2)}) copy-start(bf16[512,512]{1,0:T(8,128)(2,1)} %get-tuple-element.14) | copy-start | bytes 1572868

commit v3 on v2

--- a/solution.py
+++ b/solution.py
@@ -39,9 +39,9 @@
     tok_hbm, dout_hbm, prob_ref, routes_ref, wg_hbm, wu_hbm, wd_hbm,
     dtok_ref, dprob_ref, ggate_ref, gup_ref, gdown_ref,
     zl_ref, meta_all, meta, onehot, perm, expand, snd, rxz, wts, rows_x, rows_z, extra,
-    dall, rrcv, zsnd, zrcv, acc, core_rcv, low_rcv,
+    dall, rrcv, zsnd, zrcv, esnd, ercv, ent, acc, early, gsum, lsnd, core_rcv, low_rcv,
     load_sem, zs_sem, zr_sem, ms_sem, mr_sem, as_sem, ar_sem, bs_sem, br_sem,
-    ts_sem, tr_sem, cs_sem, cr_sem, ls_sem, lr_sem,
+    ts_sem, tr_sem, es_sem, er_sem, cs_sem, cr_sem, ls_sem, lr_sem,
 ):
     dp, ex = lax.axis_index("dp"), lax.axis_index("expert")
     core, low = lax.rem(dp, 2), lax.div(dp, 2)
@@ -98,17 +98,6 @@
         greet(column(offset))
     greet(other_core)
     greet(other_low)
-    pl.semaphore_wait(barrier, NP - 1 + 6)
-
-    def along_z(c, a):
-        remote(
-            zl_ref.at[a, jnp.where(c == 3, 1, 0)], zl_ref.at[a, c],
-            zs_sem.at[a, c - 1], zr_sem.at[a, c - 1], column(jnp.where(c == 1, -sign, 2 * sign)),
-        ).start()
-
-    loads[0].wait()
-    along_z(1, 0)
-    loads[1].wait()
 
     routes = routes_ref[...]
     rank = (routes & 3) * NP + (routes >> 2)
@@ -125,6 +114,21 @@
     for h in range(4):
         meta_all[32 * h : 32 * h + 16, :] = slot[16 * h : 16 * h + 16].astype(BF)
         meta_all[32 * h + 16 : 32 * h + 32, :] = weight[16 * h : 16 * h + 16].astype(BF)
+    row, col = iota((MAIN, MAIN), 0), iota((MAIN, MAIN), 1)
+    perm[...] = jnp.where(col == (row & 15) * 16 + (row >> 4), 1.0, 0.0).astype(BF)
+    expand[...] = jnp.where(iota((MAIN, NP), 0) >> 4 == iota((MAIN, NP), 1), 1.0, 0.0).astype(BF)
+
+    pl.semaphore_wait(barrier, NP - 1 + 6)
+
+    def along_z(c, a):
+        remote(
+            zl_ref.at[a, jnp.where(c == 3, 1, 0)], zl_ref.at[a, c],
+            zs_sem.at[a, c - 1], zr_sem.at[a, c - 1], column(jnp.where(c == 1, -sign, 2 * sign)),
+        ).start()
+
+    loads[0].wait()
+    along_z(1, 0)
+    loads[1].wait()
     for j, offset in enumerate((-sign, 2 * sign, -3 * sign)):
         there = lax.div(lax.rem(z + offset + 2 * NZ, NZ), 2)
         remote(
@@ -133,10 +137,6 @@
         ).start()
     meta[0] = meta_all[pl.ds(pl.multiple_of(high * 32, 32), 32), :]
 
-    row, col = iota((MAIN, MAIN), 0), iota((MAIN, MAIN), 1)
-    perm[...] = jnp.where(col == (row & 15) * 16 + (row >> 4), 1.0, 0.0).astype(BF)
-    expand[...] = jnp.where(iota((MAIN, NP), 0) >> 4 == iota((MAIN, NP), 1), 1.0, 0.0).astype(BF)
-
     def to_tiles(value):
         stacked = jnp.concatenate([value[:, LANE * j : LANE * (j + 1)] for j in range(16)], axis=0)
         return dot(perm[...], stacked).astype(BF)
@@ -194,41 +194,52 @@
         here = pl.ds(pl.multiple_of(c * MAIN, MAIN), MAIN)
         spare = pl.ds(pl.multiple_of(NCH * MAIN + c * NP, NP), NP)
         side = pl.ds(pl.multiple_of(c * NP, NP), NP)
-        for a, rows in ((0, rows_x), (1, rows_z)):
+
+        def arrive(a, rows):
             wait_for(rxz.at[a, c, 0:OTHERS, :], ar_sem.at[a, c])
             rows[0:MAIN, 0:D] = rxz[a, c, :, 0:D]
             for j, block in enumerate(from_tiles(rxz[a, c, :, D:WIDE])):
                 rows[MAIN:ROWS, LANE * j : LANE * (j + 1)] = block
                 extra[a, side, LANE * j : LANE * (j + 1)] = block
+
+        arrive(0, rows_x)
         gate = dot(rows_x[:, 0:QD], wts[0, 0])
         up = dot(rows_x[:, 0:QD], wts[1, 0])
-        back = dot(rows_z[:, 0:QD], wts[2, 0], 1, 1)
         for r in range(1, 4):
             part = slice(QD * r, QD * (r + 1))
             gate = gate + dot(rows_x[:, part], wts[0, r])
             up = up + dot(rows_x[:, part], wts[1, r])
-            back = back + dot(rows_z[:, part], wts[2, r], 1, 1)
         sig = jax.nn.sigmoid(gate)
         silu = gate * sig
         hidden = (silu * up).astype(BF)
+        slope = up * sig * (1.0 + gate * (1.0 - sig))
+        arrive(1, rows_z)
+        back = dot(rows_z[:, 0:QD], wts[2, 0], 1, 1)
+        for r in range(1, 4):
+            back = back + dot(rows_z[:, QD * r : QD * (r + 1)], wts[2, r], 1, 1)
         prob = jnp.sum(hidden.astype(F32) * back, axis=1, keepdims=True)
-        d_gate = (back * up * sig * (1.0 + gate * (1.0 - sig))).astype(BF)
+        d_gate = (back * slope).astype(BF)
         d_up = (back * silu).astype(BF)
         for g, value in ((0, d_gate), (1, d_up), (2, hidden)):
             dall[g, here, :] = value[0:MAIN]
             dall[g, spare, :] = value[MAIN:ROWS]
         wait_for(snd.at[0, c, 0:OTHERS, 0:WIDE], as_sem.at[0, c])
+        prob_main = jnp.broadcast_to(prob[0:MAIN], (MAIN, LANE))
+        prob_last = dot(expand[...], jnp.broadcast_to(prob[MAIN:ROWS], (NP, LANE)).astype(BF))
+        snd[0, c, :, WIDE:BACK] = jnp.where(
+            iota((MAIN, LANE), 1) < 64, prob_main, prob_last
+        ).astype(BF)
+
+    def token_rows(c):
+        here = pl.ds(pl.multiple_of(c * MAIN, MAIN), MAIN)
+        spare = pl.ds(pl.multiple_of(NCH * MAIN + c * NP, NP), NP)
+        d_gate, d_up = [jnp.concatenate([dall[g, here, :], dall[g, spare, :]]) for g in range(2)]
         tail = []
         for r in range(4):
             d_rows = (dot(d_gate, wts[0, r], 1, 1) + dot(d_up, wts[1, r], 1, 1)).astype(BF)
             snd[0, c, :, QD * r : QD * (r + 1)] = d_rows[0:MAIN]
             tail.append(d_rows[MAIN:ROWS])
         snd[0, c, :, D:WIDE] = to_tiles(jnp.concatenate(tail, axis=1))
-        prob_main = jnp.broadcast_to(prob[0:MAIN], (MAIN, LANE))
-        prob_last = dot(expand[...], jnp.broadcast_to(prob[MAIN:ROWS], (NP, LANE)).astype(BF))
-        snd[0, c, :, WIDE:BACK] = jnp.where(
-            iota((MAIN, LANE), 1) < 64, prob_main, prob_last
-        ).astype(BF)
 
     def give_back(c):
         mine = pl.ds(pl.multiple_of(me * SLOTS, SLOTS), SLOTS)
@@ -250,21 +261,19 @@
         for j, block in enumerate(from_tiles(rrcv[c, :, D:WIDE])):
             rows_x[MAIN:ROWS, LANE * j : LANE * (j + 1)] = block
         tile = rrcv[c, :, WIDE:BACK]
-        owner = iota((MAIN, LANE), 0) >> 4
-        rows_x[0:MAIN, D:WIDE] = jnp.where(
-            iota((MAIN, LANE), 1) == owner + high * NP, tile.astype(F32), 0.0
-        ).astype(BF)
+        of_slot = (onehot[c, 0, 0:MAIN, :].astype(F32) * tile[:, 0:1].astype(F32)).astype(BF)
         first = jnp.where(iota((NP, MAIN), 1) == iota((NP, MAIN), 0) * SLOTS, 1.0, 0.0).astype(BF)
-        rows_x[MAIN:ROWS, D:WIDE] = jnp.where(
-            iota((NP, LANE), 1) == iota((NP, LANE), 0) + high * NP + 64, dot(first, tile), 0.0
-        ).astype(BF)
-        return dot(onehot[c, 0], rows_x[...], 0, 0)
+        of_last = onehot[c, 0, MAIN:ROWS, :].astype(F32) * dot(first, tile)[:, 64:65]
+        entries = dot(expand[...], of_slot, 0, 0) + of_last
+        return dot(onehot[c, 0], rows_x[...], 0, 0), entries.astype(BF)
 
     def combine_far(c):
-        zsnd[c - 1] = combine(c).astype(BF)
-        remote(
-            zsnd.at[c - 1], zrcv.at[c - 1], ts_sem.at[c - 1], tr_sem.at[c - 1], column(-c * sign)
-        ).start()
+        rows, entries = combine(c)
+        zsnd[c - 1] = rows.astype(BF)
+        esnd[c - 1] = entries
+        home = column(-c * sign)
+        remote(zsnd.at[c - 1], zrcv.at[c - 1], ts_sem.at[c - 1], tr_sem.at[c - 1], home).start()
+        remote(esnd.at[c - 1], ercv.at[c - 1], es_sem.at[c - 1], er_sem.at[c - 1], home).start()
 
     dispatch(0)
     for load in loads[2:]:
@@ -279,58 +288,94 @@
         def _():
             give_back(1)
 
+        @pl.when(c == NCH - 1)
+        def _():
+            lax.fori_loop(0, 3, early_sums, 0)
+
         expert(c)
 
+        @pl.when(c < NCH - 1)
+        def _():
+            token_rows(c)
+
+        return carry
+
+    old, old_tail = (NCH - 1) * MAIN, NCH * MAIN + (NCH - 1) * NP
+
+    def width(r):
+        return pl.ds(pl.multiple_of(r * QD, QD), QD)
+
+    def early_sums(g, carry):
+        a = lax.div(g, 2)
+        for k, r in enumerate(((1 - low) * 2 + 1 - core, (1 - low) * 2 + core)):
+            rows = rxz[a, 0 : NCH - 1, :, width(r)].reshape(old, QD)
+            total = dot(dall[g, 0:old, :], rows, 0, 0)
+            early[g, k] = total + dot(
+                dall[g, NCH * MAIN : old_tail, :], extra[a, 0 : (NCH - 1) * NP, width(r)], 0, 0
+            )
+        return carry
+
+    def whole_sum(g, k, r):
+        a = lax.div(g, 2)
+        total = early[g, k] + dot(
+            dall[g, old : NCH * MAIN, :], rxz[a, NCH - 1, :, width(r)], 0, 0
+        )
+        return total + dot(
+            dall[g, old_tail : NCH * ROWS, :], extra[a, (NCH - 1) * NP : NCH * NP, width(r)], 0, 0
+        )
+
+    def full_sum(g, r):
+        a = lax.div(g, 2)
+        rows = rxz[a, :, :, width(r)].reshape(NCH * MAIN, QD)
+        total = dot(dall[g, 0 : NCH * MAIN, :], rows, 0, 0)
+        return total + dot(dall[g, NCH * MAIN : NCH * ROWS, :], extra[a, :, width(r)], 0, 0)
+
+    def to_core(g, half, total):
+        gsum[g, half] = total.astype(BF)
+        remote(
+            gsum.at[g, half], core_rcv.at[g, half],
+            cs_sem.at[g, half], cr_sem.at[g, half], other_core,
+        ).start()
+
+    def far_half(g, carry):
+        to_core(g, 1 - low, whole_sum(g, 0, (1 - low) * 2 + 1 - core))
+        return carry
+
+    def to_low(g, carry):
+        total = whole_sum(g, 1, (1 - low) * 2 + core)
+        wait_for(core_rcv.at[g, 1 - low], cr_sem.at[g, 1 - low])
+        lsnd[g] = (total + core_rcv[g, 1 - low].astype(F32)).astype(BF)
+        remote(lsnd.at[g], low_rcv.at[g], ls_sem.at[g], lr_sem.at[g], other_low).start()
+        return carry
+
+    def near_half(g, carry):
+        to_core(g, low, full_sum(g, low * 2 + 1 - core))
         return carry
 
     lax.fori_loop(0, NCH, step, 0)
+    lax.fori_loop(0, 3, far_half, 0)
+    lax.fori_loop(0, 3, to_low, 0)
+    token_rows(NCH - 1)
     for c in (3, 2, 0):
         give_back(c)
-
-    def weight_gradient(g, r):
-        a = lax.div(g, 2)
-        part = pl.ds(pl.multiple_of(r * QD, QD), QD)
-        main = dall[g, 0 : NCH * MAIN, :]
-        total = dot(main, rxz[a, :, :, part].reshape(NCH * MAIN, QD), 0, 0)
-        total = total + dot(dall[g, NCH * MAIN : NCH * ROWS, :], extra[a, :, part], 0, 0)
-        wts[g, r] = total.astype(BF)
-
-    def to_core(i, carry):
-        g, half = lax.div(i, 2), lax.rem(i, 2)
-        r = half * 2 + 1 - core
-        weight_gradient(g, r)
-        remote(
-            wts.at[g, r], core_rcv.at[g, half], cs_sem.at[g, half], cr_sem.at[g, half], other_core
-        ).start()
-        return carry
-
-    lax.fori_loop(0, 6, to_core, 0)
-
-    def to_low(g, carry):
-        r = (1 - low) * 2 + core
-        weight_gradient(g, r)
-        wait_for(core_rcv.at[g, 1 - low], cr_sem.at[g, 1 - low])
-        wts[g, r] = (wts[g, r].astype(F32) + core_rcv[g, 1 - low].astype(F32)).astype(BF)
-        remote(wts.at[g, r], low_rcv.at[g], ls_sem.at[g], lr_sem.at[g], other_low).start()
-        return carry
-
-    lax.fori_loop(0, 3, to_low, 0)
+    lax.fori_loop(0, 3, near_half, 0)
     combine_far(1)
 
     def to_own(g, carry):
-        weight_gradient(g, low * 2 + core)
+        early[g, 0] = full_sum(g, low * 2 + core)
         return carry
 
     lax.fori_loop(0, 3, to_own, 0)
     combine_far(3)
     combine_far(2)
-    acc[...] = combine(0)
+    rows, entries = combine(0)
+    acc[...] = rows
+    ent[pl.ds(pl.multiple_of(high * NP, NP), NP), :] = entries
 
     def finish(g):
         wait_for(core_rcv.at[g, low], cr_sem.at[g, low])
         wait_for(low_rcv.at[g], lr_sem.at[g])
-        own = wts[g, low * 2 + core].astype(F32)
-        return own + core_rcv[g, low].astype(F32) + low_rcv[g].astype(F32)
+        return early[g, 0] + core_rcv[g, low].astype(F32) + low_rcv[g].astype(F32)
 
     ggate_ref[...] = finish(0).T.astype(BF)
     gup_ref[...] = finish(1).T.astype(BF)
@@ -340,9 +385,12 @@
     total = acc[...]
     for j in range(NCH - 1):
         total = total + zrcv[j].astype(F32)
-    dtok_ref[...] = total[:, 0:D].astype(BF)
-    entries = total[:, D:WIDE].T
-    entries = entries[0:64] + entries[64:LANE]
+    dtok_ref[...] = total.astype(BF)
+    for j, offset in enumerate((-sign, 2 * sign, -3 * sign)):
+        there = lax.div(lax.rem(z + offset + 2 * NZ, NZ), 2)
+        wait_for(ercv.at[j], er_sem.at[j])
+        ent[pl.ds(pl.multiple_of(there * NP, NP), NP), :] = ercv[j]
+    entries = ent[...].astype(F32)
     d_probs = jnp.zeros((TOP, T), F32)
     for k in range(TOP):
         entry = jnp.sum(
@@ -356,6 +404,7 @@
             wait_for(zl_ref.at[a, 0], zs_sem.at[a, j])
         wait_for(meta.at[0], ms_sem.at[j])
         wait_for(zsnd.at[j], ts_sem.at[j])
+        wait_for(esnd.at[j], es_sem.at[j])
     for c in range(NCH):
         wait_for(snd.at[1, c, 0:OTHERS, 0:WIDE], as_sem.at[1, c])
         wait_for(snd.at[0, c, 0:OTHERS, :], bs_sem.at[c])
@@ -389,20 +438,26 @@
             pltpu.VMEM((2, NCH, MAIN, BACK), BF),
             pltpu.VMEM((2, NCH, MAIN, WIDE), BF),
             pltpu.VMEM((3, 4, F, QD), BF),
-            pltpu.VMEM((ROWS, WIDE), BF),
+            pltpu.VMEM((ROWS, D), BF),
             pltpu.VMEM((ROWS, D), BF),
             pltpu.VMEM((2, NCH * NP, D), BF),
             pltpu.VMEM((3, NCH * ROWS, F), BF),
             pltpu.VMEM((NCH, MAIN, BACK), BF),
-            pltpu.VMEM((NCH - 1, T, WIDE), BF),
-            pltpu.VMEM((NCH - 1, T, WIDE), BF),
-            pltpu.VMEM((T, WIDE), F32),
+            pltpu.VMEM((NCH - 1, T, D), BF),
+            pltpu.VMEM((NCH - 1, T, D), BF),
+            pltpu.VMEM((NCH - 1, NP, T), BF),
+            pltpu.VMEM((NCH - 1, NP, T), BF),
+            pltpu.VMEM((4 * NP, T), BF),
+            pltpu.VMEM((T, D), F32),
+            pltpu.VMEM((3, 2, F, QD), F32),
+            pltpu.VMEM((3, 2, F, QD), BF),
+            pltpu.VMEM((3, F, QD), BF),
             pltpu.VMEM((3, 2, F, QD), BF),
             pltpu.VMEM((3, F, QD), BF),
             dma((8,)),
             dma((2, 3)), dma((2, 3)), dma((3,)), dma((3,)),
             dma((2, NCH)), dma((2, NCH)), dma((NCH,)), dma((NCH,)),
-            dma((3,)), dma((3,)), dma((3, 2)), dma((3, 2)), dma((3,)), dma((3,)),
+            dma((3,)), dma((3,)), dma((3,)), dma((3,)), dma((3, 2)), dma((3, 2)), dma((3,)), dma((3,)),
         ],
         compiler_params=pltpu.CompilerParams(
             collective_id=0, has_side_effects=True, vmem_limit_bytes=62 << 20

time: 201 us -> 194 us (0.965)
  the two profiles are of different devices: /device:TPU:54 before, /device:TPU:1 now
where the time goes in v3:
time: 194 us
  Pallas kernels  186 us (96%)
  local copies, waits for them, and re-layouts  6.68 us (3%)
    pallas_call x1, Pallas kernels, shards(): pl.pallas_call(kernel, out_shape=(jax.ShapeDtypeStruct((T, D), BF), jax.S...  186 us
    unnamed x9, local copies, waits for them, and re-layouts  6.68 us

profile of v3, /device:TPU:1, one launch (start us, length us, event | category | flops | bytes accessed | tf_op | source)
XLA Modules:
  0.0 193.5 jit_solution(17319763004816131540)
XLA Ops:
  0.6 186.2 %shard_map.110 = (bf16[128,2048]{1,0:T(8,128)(2,1)}, bf16[8,128]{1,0:T(8,128)(2,1)}, bf16[512,512]{1,0:T(8,128)(2,1)}, bf16[512,512]{1,0:T(8,128)(2,1)}, bf16[512,512]{1,0:T(8,128)(2,1)}) custom-call(bf16[128,2048]{1,0:T(8,128)(2,1)} %tok_hbm.1, bf16[128,2048]{1,0:T(8,128)(2,1)} %dout_hbm.1, bf16[8,128]{1,0:T(8,128)(2,1)} %bitcast.17, s32[8,128]{1,0:T(8,128)} %bitcast.15, ...), custom_call_target="tpu_custom_call" | custom-call | tf_op jit(solution)/shard_map/pallas_call | solution.py:420
  186.8 0.0 copy-start.1
  186.8 0.0 copy-start
  186.8 2.0 %copy.17 = bf16[128,2048]{1,0:T(8,128)(2,1)} copy(bf16[128,2048]{1,0:T(8,128)(2,1)} %get-tuple-element.20) | data formatting | bytes 1048576
  188.8 1.3 copy.18
  190.1 1.9 copy.19
  191.9 0.0 copy-done.1
  191.9 0.8 copy.20
  192.7 0.0 copy-done
  192.7 0.8 copy.21
Async XLA Ops:
  186.8 5.1 %copy-start.1 = (bf16[512,512]{1,0:T(8,128)(2,1)S(1)}, bf16[512,512]{1,0:T(8,128)(2,1)}, u32[]{:S(2)}) copy-start(bf16[512,512]{1,0:T(8,128)(2,1)} %get-tuple-element.13) | copy-start | bytes 1572868
  186.8 5.9 %copy-start = (bf16[512,512]{1,0:T(8,128)(2,1)S(1)}, bf16[512,512]{1,0:T(8,128)(2,1)}, u32[]{:S(2)}) copy-start(bf16[512,512]{1,0:T(8,128)(2,1)} %get-tuple-element.14) | copy-start | bytes 1572868

commit v4 on v3

--- a/solution.py
+++ b/solution.py
@@ -37,7 +37,7 @@
 
 def kernel(
     tok_hbm, dout_hbm, prob_ref, routes_ref, wg_hbm, wu_hbm, wd_hbm,
-    dtok_ref, dprob_ref, ggate_ref, gup_ref, gdown_ref,
+    dtok_ref, dprob_ref, grad_ref,
     zl_ref, meta_all, meta, onehot, perm, expand, snd, rxz, wts, rows_x, rows_z, extra,
     dall, rrcv, zsnd, zrcv, esnd, ercv, ent, acc, early, gsum, lsnd, core_rcv, low_rcv,
     load_sem, zs_sem, zr_sem, ms_sem, mr_sem, as_sem, ar_sem, bs_sem, br_sem,
@@ -330,15 +330,15 @@
         total = dot(dall[g, 0 : NCH * MAIN, :], rows, 0, 0)
         return total + dot(dall[g, NCH * MAIN : NCH * ROWS, :], extra[a, :, width(r)], 0, 0)
 
-    def to_core(g, half, total):
-        gsum[g, half] = total.astype(BF)
+    def to_core(g, half, place, total):
+        place[...] = total.astype(BF)
         remote(
-            gsum.at[g, half], core_rcv.at[g, half],
+            place, core_rcv.at[g, half],
             cs_sem.at[g, half], cr_sem.at[g, half], other_core,
         ).start()
 
     def far_half(g, carry):
-        to_core(g, 1 - low, whole_sum(g, 0, (1 - low) * 2 + 1 - core))
+        to_core(g, 1 - low, gsum.at[g], whole_sum(g, 0, (1 - low) * 2 + 1 - core))
         return carry
 
     def to_low(g, carry):
@@ -349,7 +349,7 @@
         return carry
 
     def near_half(g, carry):
-        to_core(g, low, full_sum(g, low * 2 + 1 - core))
+        to_core(g, low, wts.at[g, 0], full_sum(g, low * 2 + 1 - core))
         return carry
 
     lax.fori_loop(0, NCH, step, 0)
@@ -369,7 +369,8 @@
     combine_far(3)
     combine_far(2)
     rows, entries = combine(0)
-    acc[...] = rows
+    wait_for(zrcv.at[0], tr_sem.at[0])
+    acc[...] = rows + zrcv[0].astype(F32)
     ent[pl.ds(pl.multiple_of(high * NP, NP), NP), :] = entries
 
     def finish(g):
@@ -377,15 +378,12 @@
         wait_for(low_rcv.at[g], lr_sem.at[g])
         return early[g, 0] + core_rcv[g, low].astype(F32) + low_rcv[g].astype(F32)
 
-    ggate_ref[...] = finish(0).T.astype(BF)
-    gup_ref[...] = finish(1).T.astype(BF)
-    gdown_ref[...] = finish(2).astype(BF)
-    for j in range(NCH - 1):
+    grad_ref[0] = finish(0).T.astype(BF)
+    grad_ref[1] = finish(1).T.astype(BF)
+    grad_ref[2] = finish(2).astype(BF)
+    for j in (2, 1):
         wait_for(zrcv.at[j], tr_sem.at[j])
-    total = acc[...]
-    for j in range(NCH - 1):
-        total = total + zrcv[j].astype(F32)
-    dtok_ref[...] = total.astype(BF)
+    dtok_ref[...] = (acc[...] + zrcv[2].astype(F32) + zrcv[1].astype(F32)).astype(BF)
     for j, offset in enumerate((-sign, 2 * sign, -3 * sign)):
         there = lax.div(lax.rem(z + offset + 2 * NZ, NZ), 2)
         wait_for(ercv.at[j], er_sem.at[j])
@@ -417,17 +415,15 @@
 def shards(tokens, d_out, route_probs, routes, w_gate, w_up, w_down):
     dma = pltpu.SemaphoreType.DMA
     anywhere, vmem = pl.BlockSpec(memory_space=pl.ANY), pl.BlockSpec(memory_space=pltpu.VMEM)
-    d_tokens, d_probs, g_gate, g_up, g_down = pl.pallas_call(
+    d_tokens, d_probs, grads = pl.pallas_call(
         kernel,
         out_shape=(
             jax.ShapeDtypeStruct((T, D), BF),
             jax.ShapeDtypeStruct((TOP, T), BF),
-            jax.ShapeDtypeStruct((QD, F), BF),
-            jax.ShapeDtypeStruct((QD, F), BF),
-            jax.ShapeDtypeStruct((F, QD), BF),
+            jax.ShapeDtypeStruct((3, F, QD), BF),
         ),
         in_specs=[anywhere, anywhere, vmem, vmem, anywhere, anywhere, anywhere],
-        out_specs=(vmem, vmem, vmem, vmem, vmem),
+        out_specs=(vmem, vmem, vmem),
         scratch_shapes=[
             pltpu.VMEM((2, NCH, T, D), BF),
             pltpu.VMEM((T, LANE), BF),
@@ -450,7 +446,7 @@
             pltpu.VMEM((4 * NP, T), BF),
             pltpu.VMEM((T, D), F32),
             pltpu.VMEM((3, 2, F, QD), F32),
-            pltpu.VMEM((3, 2, F, QD), BF),
+            pltpu.VMEM((3, F, QD), BF),
             pltpu.VMEM((3, F, QD), BF),
             pltpu.VMEM((3, 2, F, QD), BF),
             pltpu.VMEM((3, F, QD), BF),
@@ -469,9 +465,9 @@
     return (
         d_tokens,
         d_probs.T,
-        g_gate[None],
-        g_up[None],
-        g_down[None],
+        grads[0:1],
+        grads[1:2],
+        grads[2:3],
     )
 
 

time: 194 us -> 191 us (0.985)
  local copies, waits for them, and re-layouts: 6.68 us -> 3.97 us
    unnamed x9 -> x6, local copies, waits for them, and re-layouts: 6.68 us -> 1.38 us
    slice x0 -> x1, local copies, waits for them, and re-layouts: none -> 2.59 us  [shards(): return (d_tokens, d_probs.T, grads[0:1], grads[1:2], grads[2:3])]
where the time goes in v4:
time: 191 us
  Pallas kernels  186 us (97%)
  local copies, waits for them, and re-layouts  3.97 us (2%)
    pallas_call x1, Pallas kernels, shards(): pl.pallas_call(kernel, out_shape=(jax.ShapeDtypeStruct((T, D), BF), jax.S...  186 us

profile of v4, /device:TPU:1, one launch (start us, length us, event | category | flops | bytes accessed | tf_op | source)
XLA Modules:
  0.0 190.6 jit_solution(17181497338886129707)
XLA Ops:
  0.6 186.0 %shard_map.110 = (bf16[128,2048]{1,0:T(8,128)(2,1)}, bf16[8,128]{1,0:T(8,128)(2,1)}, bf16[3,512,512]{2,1,0:T(8,128)(2,1)}) custom-call(bf16[128,2048]{1,0:T(8,128)(2,1)} %tok_hbm.1, bf16[128,2048]{1,0:T(8,128)(2,1)} %dout_hbm.1, bf16[8,128]{1,0:T(8,128)(2,1)} %bitcast.11, s32[8,128]{1,0:T(8,128)} %bitcast.9, bf16[4,512,512]{2,1,0:T(8,128)(2,1)} %bitcast.6, ...), custom_call_target="tpu_custom_call" | custom-call | tf_op jit(solution)/shard_map/pallas_call | solution.py:418
  186.6 0.0 copy-start
  186.7 0.0 copy-start.1
  186.7 2.6 %fusion = (bf16[1,512,512]{2,1,0:T(8,128)(2,1)}, bf16[1,512,512]{2,1,0:T(8,128)(2,1)}, bf16[1,512,512]{2,1,0:T(8,128)(2,1)}) fusion(bf16[3,512,512]{2,1,0:T(8,128)(2,1)} %get-tuple-element.10), kind=kLoop, calls=%fused_computation | loop fusion | bytes 3145728 | tf_op jit(solution)/shard_map/slice | solution.py:470
  189.2 0.0 copy-done
  189.2 0.8 copy.14
  190.0 0.0 copy-done.1
  190.0 0.6 copy.15
Async XLA Ops:
  186.6 2.6 %copy-start = (bf16[128,2048]{1,0:T(8,128)(2,1)S(1)}, bf16[128,2048]{1,0:T(8,128)(2,1)}, u32[]{:S(2)}) copy-start(bf16[128,2048]{1,0:T(8,128)(2,1)} %get-tuple-element.19) | copy-start | bytes 1572868
  186.7 3.4 %copy-start.1 = (bf16[8,128]{1,0:T(8,128)(2,1)S(1)}, bf16[8,128]{1,0:T(8,128)(2,1)}, u32[]{:S(2)}) copy-start(bf16[8,128]{1,0:T(8,128)(2,1)} %get-tuple-element.9) | copy-start | bytes 6148

commit v5 on v4

--- a/solution.py
+++ b/solution.py
@@ -353,20 +353,32 @@
         return carry
 
     lax.fori_loop(0, NCH, step, 0)
-    lax.fori_loop(0, 3, far_half, 0)
-    lax.fori_loop(0, 3, to_low, 0)
+    def far_then_low(g, carry):
+        @pl.when(g < 3)
+        def _():
+            far_half(g, 0)
+
+        @pl.when(g >= 1)
+        def _():
+            to_low(g - 1, 0)
+
+        return carry
+
+    lax.fori_loop(0, 2, far_then_low, 0)
     token_rows(NCH - 1)
-    for c in (3, 2, 0):
+    give_back(3)
+    lax.fori_loop(2, 4, far_then_low, 0)
+    combine_far(1)
+    for c in (2, 0):
         give_back(c)
     lax.fori_loop(0, 3, near_half, 0)
-    combine_far(1)
 
     def to_own(g, carry):
         early[g, 0] = full_sum(g, low * 2 + core)
         return carry
 
+    combine_far(3)
     lax.fori_loop(0, 3, to_own, 0)
-    combine_far(3)
     combine_far(2)
     rows, entries = combine(0)
     wait_for(zrcv.at[0], tr_sem.at[0])

time: 191 us -> 189 us (0.990)
  Pallas kernels: 186 us -> 184 us
    pallas_call x1, Pallas kernels: 186 us -> 184 us  [shards(): pl.pallas_call(kernel, out_shape=(jax.ShapeDtypeStruct((T, D), BF), jax.S...]
where the time goes in v5:
time: 189 us
  Pallas kernels  184 us (97%)
  local copies, waits for them, and re-layouts  3.97 us (2%)
    pallas_call x1, Pallas kernels, shards(): pl.pallas_call(kernel, out_shape=(jax.ShapeDtypeStruct((T, D), BF), jax.S...  184 us

profile of v5, /device:TPU:1, one launch (start us, length us, event | category | flops | bytes accessed | tf_op | source)
XLA Modules:
  0.0 188.7 jit_solution(1681651059896637256)
XLA Ops:
  0.6 184.1 %shard_map.110 = (bf16[128,2048]{1,0:T(8,128)(2,1)}, bf16[8,128]{1,0:T(8,128)(2,1)}, bf16[3,512,512]{2,1,0:T(8,128)(2,1)}) custom-call(bf16[128,2048]{1,0:T(8,128)(2,1)} %tok_hbm.1, bf16[128,2048]{1,0:T(8,128)(2,1)} %dout_hbm.1, bf16[8,128]{1,0:T(8,128)(2,1)} %bitcast.11, s32[8,128]{1,0:T(8,128)} %bitcast.9, bf16[4,512,512]{2,1,0:T(8,128)(2,1)} %bitcast.6, ...), custom_call_target="tpu_custom_call" | custom-call | tf_op jit(solution)/shard_map/pallas_call | solution.py:430
  184.7 0.0 copy-start
  184.7 0.0 copy-start.1
  184.7 2.6 %fusion = (bf16[1,512,512]{2,1,0:T(8,128)(2,1)}, bf16[1,512,512]{2,1,0:T(8,128)(2,1)}, bf16[1,512,512]{2,1,0:T(8,128)(2,1)}) fusion(bf16[3,512,512]{2,1,0:T(8,128)(2,1)} %get-tuple-element.10), kind=kLoop, calls=%fused_computation | loop fusion | bytes 3145728 | tf_op jit(solution)/shard_map/slice | solution.py:482
  187.3 0.0 copy-done
  187.3 0.8 copy.14
  188.1 0.0 copy-done.1
  188.1 0.6 copy.15
Async XLA Ops:
  184.7 2.6 %copy-start = (bf16[128,2048]{1,0:T(8,128)(2,1)S(1)}, bf16[128,2048]{1,0:T(8,128)(2,1)}, u32[]{:S(2)}) copy-start(bf16[128,2048]{1,0:T(8,128)(2,1)} %get-tuple-element.19) | copy-start | bytes 1572868
  184.7 3.4 %copy-start.1 = (bf16[8,128]{1,0:T(8,128)(2,1)S(1)}, bf16[8,128]{1,0:T(8,128)(2,1)}, u32[]{:S(2)}) copy-start(bf16[8,128]{1,0:T(8,128)(2,1)} %get-tuple-element.9) | copy-start | bytes 6148
